TPU v7x, 256 devices: a whole 4x4x8 slice. The times are simulated.
256 devices in a mesh: row: 16 (over z_hi, x, core), col: 16 (over y, z_lo).
Axes of the slice: x: 4, y: 4, z: 8 (z_hi: 2, z_lo: 4; z = z_hi * 4 + z_lo), core: 2. Of those that a mesh axis runs over, the one named last changes fastest.
Arguments:
- pair: bfloat16 [576, 576, 128], P('row', 'col'), may hold values from -6 to 6
- cotangent: bfloat16 [576, 576, 128], P('row', 'col'), may hold values from -6 to 6
- gain_in: float32 [128], replicated, may hold values from 0.25 to 1.75
- bias_in: float32 [128], replicated, may hold values from -3 to 3
- w_in: bfloat16 [128, 640], replicated, may hold values from -0.5 to 0.5
- gain_out: float32 [128], replicated, may hold values from 0.25 to 1.75
- bias_out: float32 [128], replicated, may hold values from -3 to 3
- w_out: bfloat16 [128, 128], replicated, may hold values from -0.5 to 0.5
Outputs:
- update: bfloat16 [576, 576, 128], P('row', 'col')
- pair_grad: bfloat16 [576, 576, 128], P('row', 'col')
All inputs are finite; a program needn't handle non-finite values.
Results may differ from a plain program's by a relative error of at most 0.023.
Values may be sent and summed in bfloat16 or wider, within the bound.
No kernel may reach another device: no remote copies, remote signals or barrier semaphores. Data moves between devices by JAX's collectives and lax.ppermute only.
A program may use at most 128 MiB of HBM per device.

v0:
```python
import jax
import jax.numpy as jnp
from jax import lax
from jax.experimental import pallas as pl
from jax.experimental.pallas import tpu as pltpu
from jax.sharding import Mesh, PartitionSpec as P

EPS = 1e-05
BF = jnp.bfloat16
F32 = jnp.float32

TILE = 36
SLOT = 40
SLOTS = 3
GROUPS = 12
LANES = 128
ROWS = 16
PART = 4
PARTS = GROUPS // PART
CH = 128
NB = 8
KB = 16
KG = 6
JG = 3
CHUNKS = 4
NAMES = ("zh", "x", "core", "y", "zl")
WIDE = ("zh", "x", "y", "zl")


def params(mib=14):
    return pltpu.CompilerParams(vmem_limit_bytes=mib * 1024 * 1024)


def dot(a, b, ca, cb):
    return lax.dot_general(a, b, (((ca,), (cb,)), ((), ())), preferred_element_type=F32)


def used_lanes(shape):
    lane = lax.broadcasted_iota(jnp.int32, shape, len(shape) - 1)
    used = lane < TILE
    for s in range(1, SLOTS):
        used = used | ((lane >= SLOT * s) & (lane < SLOT * s + TILE))
    return used


def swap_slots(blocks):
    shape = next(b.shape for b in blocks if b is not None)
    lane = lax.broadcasted_iota(jnp.int32, shape, 1)
    out = []
    for s in range(SLOTS):
        acc = jnp.zeros(shape, F32)
        for q, b in enumerate(blocks):
            if b is None:
                continue
            shift = (SLOT * (q - s)) % LANES
            moved = pltpu.roll(b, shift, 1) if shift else b
            acc = jnp.where((lane >= SLOT * q) & (lane < SLOT * (q + 1)), moved, acc)
        out.append(acc)
    return out


def spread_tile(tile_ref, scr):
    for r in range(GROUPS):
        for s in range(SLOTS):
            scr[r, SLOT * s : SLOT * s + TILE, :] = tile_ref[r + GROUPS * s].astype(F32)


def gather_tile(value, tile_ref, r):
    for s in range(SLOTS):
        tile_ref[r + GROUPS * s] = value[SLOT * s : SLOT * s + TILE].astype(BF)


def send_tile(tile_ref, tile_hbm, r, sems):
    if r % PART < PART - 1:
        return []
    copies = []
    for s in range(SLOTS):
        rows = pl.ds(r + 1 - PART + GROUPS * s, PART)
        copies.append(pltpu.make_async_copy(tile_ref.at[rows], tile_hbm.at[rows], sems.at[r // PART * SLOTS + s]))
        copies[-1].start()
    return copies


def normalized(x, axis):
    center = x - jnp.mean(x, axis, keepdims=True)
    scale = lax.rsqrt(jnp.mean(center * center, axis, keepdims=True) + EPS)
    return center * scale, scale


def norm_grad(d, xhat, scale, axis):
    return scale * (d - jnp.mean(d, axis, keepdims=True) - xhat * jnp.mean(d * xhat, axis, keepdims=True))


def message(leading, arrays=1):
    return jax.ShapeDtypeStruct(leading + (PART, arrays * PARTS * LANES), BF)


def part_lanes(p):
    return slice(LANES * p, LANES * (p + 1))


def row_at(r):
    return pl.ds(r // PART * CH * 8 + r % PART, CH, stride=8)


def by_row(scr):
    return scr.reshape(PARTS * CH * 8, LANES)


PADDED = pltpu.VMEM((PARTS, CH, 8, LANES), F32)


def pack(out_ref, scr, array=0, rows=slice(None)):
    for p in range(PARTS):
        out_ref[rows, :, part_lanes(array * PARTS + p)] = scr[p, rows, :PART, :].astype(BF)


def unpack(in_ref, scr, array=0):
    for p in range(PARTS):
        scr[p, :, :PART, :] = in_ref[:, :, part_lanes(array * PARTS + p)].astype(F32)


def read_rows(in_ref, scr, array=0):
    scr[:, :, GROUPS:, :] = jnp.zeros((NB, KB, ROWS - GROUPS, LANES), scr.dtype)
    for p in range(PARTS):
        scr[:, :, PART * p : PART * (p + 1), :] = in_ref[:, :, :, part_lanes(array * PARTS + p)].astype(scr.dtype)


def write_rows(out_ref, at, value, scr):
    scr[...] = value.astype(scr.dtype).reshape(NB, ROWS, LANES)
    for p in range(PARTS):
        out_ref[:, at, :, part_lanes(p)] = scr[:, PART * p : PART * (p + 1), :].astype(BF)


def column(row):
    return jnp.broadcast_to(row, (8, CH)).T[:, :1]


def fetch(sources, buffers, sems):
    copies = [pltpu.make_async_copy(s, b, sems.at[n]) for n, (s, b) in enumerate(zip(sources, buffers))]
    for copy in copies:
        copy.start()
    return copies


def in_hbm(n):
    return [pl.BlockSpec(memory_space=pltpu.HBM)] * n


def keep_in_hbm(*arrays):
    return [pltpu.with_memory_space_constraint(a, pltpu.HBM) for a in arrays]


def edges_kernel(
    pair_hbm, w_hbm, gain_hbm, bias_hbm, out_hbm,
    pair_ref, w_ref, gain_ref, bias_ref, x_scr, l_scr, r_scr, wt_scr, out_ref, sems, out_sems,
):
    copies = fetch(
        (pair_hbm, w_hbm, gain_hbm, bias_hbm), (pair_ref, w_ref, gain_ref, bias_ref), sems
    )
    x_scr[...] = jnp.zeros(x_scr.shape, F32)
    used = used_lanes((CH, LANES))
    copies[1].wait()
    wt_scr[...] = w_ref[:, : 4 * CH].astype(F32).T.astype(BF)
    copies[2].wait()
    copies[3].wait()
    copies[0].wait()
    spread_tile(pair_ref, x_scr)
    for r in range(0, GROUPS, 2):
        xhat, _ = normalized(x_scr[r : r + 2].reshape(2 * LANES, CH), 1)
        normed = (xhat * gain_ref[...] + bias_ref[...]).astype(BF)
        proj = dot(wt_scr[...], normed, 1, 1)
        left = jax.nn.sigmoid(proj[:CH]) * proj[CH : 2 * CH]
        right = jax.nn.sigmoid(proj[2 * CH : 3 * CH]) * proj[3 * CH :]
        for n in (r, r + 1):
            by_row(l_scr)[row_at(n), :] = jnp.where(used, left[:, part_lanes(n - r)], 0.0)
            by_row(r_scr)[row_at(n), :] = jnp.where(used, right[:, part_lanes(n - r)], 0.0)
    copies = []
    for n in range(CHUNKS):
        rows = slice(CH // CHUNKS * n, CH // CHUNKS * (n + 1))
        pack(out_ref, l_scr, 0, rows)
        pack(out_ref, r_scr, 1, rows)
        copies.append(pltpu.make_async_copy(out_ref.at[rows], out_hbm.at[rows], out_sems.at[n]))
        copies[-1].start()
    for copy in copies:
        copy.wait()


def edges(pair, w_in, gain_in, bias_in):
    return pl.pallas_call(
        edges_kernel,
        out_shape=message((CH,), 2),
        in_specs=in_hbm(4),
        out_specs=pl.BlockSpec(memory_space=pltpu.HBM),
        scratch_shapes=[
            pltpu.VMEM((TILE, TILE, CH), BF),
            pltpu.VMEM((CH, 5 * CH), BF),
            pltpu.VMEM((1, CH), F32),
            pltpu.VMEM((1, CH), F32),
            pltpu.VMEM((GROUPS, LANES, CH), F32),
            PADDED,
            PADDED,
            pltpu.VMEM((4 * CH, CH), BF),
            pltpu.VMEM((CH, PART, 2 * PARTS * LANES), BF),
            pltpu.SemaphoreType.DMA((4,)),
            pltpu.SemaphoreType.DMA((CHUNKS,)),
        ],
        compiler_params=params(),
        cost_estimate=pl.CostEstimate(flops=200_000_000, bytes_accessed=1_200_000, transcendentals=400_000),
        name="edges",
    )(*keep_in_hbm(pair, w_in, gain_in, bias_in))


def side_kernel(
    pair_hbm, cot_hbm, w_hbm, w_out_hbm, gain_hbm, bias_hbm, gain_out_hbm, bias_out_hbm,
    gate_ref, slope_ref, dx_ref, fac_ref, xhat_ref, scale_ref, cols_ref, w_ref, w_out_t_ref,
    pair_ref, cot_ref, w_out_ref, rows_ref, x_scr, c_scr, wt_scr, sems,
):
    copies = fetch(
        (pair_hbm, cot_hbm, w_hbm, w_out_hbm, gain_hbm, bias_hbm, gain_out_hbm, bias_out_hbm),
        (pair_ref, cot_ref, w_ref, w_out_ref) + tuple(rows_ref.at[n] for n in range(4)),
        sems,
    )
    x_scr[...] = jnp.zeros(x_scr.shape, F32)
    c_scr[...] = jnp.zeros(c_scr.shape, F32)
    scale_ref[...] = jnp.zeros(scale_ref.shape, F32)
    cols_ref[...] = jnp.zeros(cols_ref.shape, F32)
    for copy in copies:
        copy.wait()
    wt_scr[...] = w_ref[...].astype(F32).T.astype(BF)
    w_out_t_ref[...] = w_out_ref[...].astype(F32).T.astype(BF)
    gain_in, bias_in, gain_out, bias_out = (column(rows_ref[n]) for n in range(4))
    cols_ref[:, 0:1] = gain_in
    cols_ref[:, 1:2] = gain_out
    cols_ref[:, 2:3] = bias_out
    spread_tile(pair_ref, x_scr)
    spread_tile(cot_ref, c_scr)
    for r in range(GROUPS):
        xhat, scale = normalized(x_scr[r].T, 0)
        normed = (xhat * gain_in + bias_in).astype(BF)
        xhat_ref[r] = xhat
        scale_ref[r : r + 1, :] = scale
        proj = dot(wt_scr[...], normed, 1, 0)
        for h in range(2):
            sig = jax.nn.sigmoid(proj[2 * h * CH : (2 * h + 1) * CH])
            value = proj[(2 * h + 1) * CH : (2 * h + 2) * CH]
            fac_ref[r, 2 * h * CH : (2 * h + 1) * CH, :] = (value * sig * (1.0 - sig)).astype(BF)
            fac_ref[r, (2 * h + 1) * CH : (2 * h + 2) * CH, :] = sig.astype(BF)
        gate = jax.nn.sigmoid(proj[4 * CH :])
        gated = c_scr[r].T * gate
        gate_ref[r] = gate
        slope_ref[r] = gated * (1.0 - gate)
        dx_ref[r] = dot(w_out_ref[...], gated.astype(BF), 1, 0) * gain_out


def side(pair, cotangent, w_in, w_out, gain_in, bias_in, gain_out, bias_out):
    square = jax.ShapeDtypeStruct((GROUPS, CH, LANES), F32)
    return pl.pallas_call(
        side_kernel,
        out_shape=[
            square,
            square,
            square,
            jax.ShapeDtypeStruct((GROUPS, 4 * CH, LANES), BF),
            square,
            jax.ShapeDtypeStruct((ROWS, LANES), F32),
            jax.ShapeDtypeStruct((CH, LANES), F32),
            jax.ShapeDtypeStruct((CH, 5 * CH), BF),
            jax.ShapeDtypeStruct((CH, CH), BF),
        ],
        in_specs=in_hbm(8),
        scratch_shapes=[
            pltpu.VMEM((TILE, TILE, CH), BF),
            pltpu.VMEM((TILE, TILE, CH), BF),
            pltpu.VMEM((CH, CH), BF),
            pltpu.VMEM((4, 1, CH), F32),
            pltpu.VMEM((GROUPS, LANES, CH), F32),
            pltpu.VMEM((GROUPS, LANES, CH), F32),
            pltpu.VMEM((5 * CH, CH), BF),
            pltpu.SemaphoreType.DMA((8,)),
        ],
        compiler_params=params(),
        cost_estimate=pl.CostEstimate(flops=300_000_000, bytes_accessed=6_000_000, transcendentals=600_000),
        name="side",
    )(*keep_in_hbm(pair, cotangent, w_in, w_out, gain_in, bias_in, gain_out, bias_out))


def assemble_left_kernel(in_ref, left_ref, t_scr):
    read_rows(in_ref, t_scr)
    for g in range(KG):
        blocks = [
            t_scr[:, SLOTS * g + q].astype(F32).reshape(CH, LANES) if SLOTS * g + q < KB else None
            for q in range(SLOTS)
        ]
        for s, value in enumerate(swap_slots(blocks)):
            left_ref[CH * s : CH * (s + 1), part_lanes(g)] = value.astype(BF)


def assemble_left(received):
    return pl.pallas_call(
        assemble_left_kernel,
        out_shape=jax.ShapeDtypeStruct((SLOTS * NB * ROWS, KG * LANES), BF),
        scratch_shapes=[pltpu.VMEM((NB, KB, ROWS, LANES), BF)],
        compiler_params=params(),
        cost_estimate=pl.CostEstimate(flops=2_000_000, bytes_accessed=1_000_000, transcendentals=0),
        name="assemble_left",
    )(received.reshape(NB, KB, PART, 2 * PARTS * LANES))


def assemble_right_kernel(in_ref, right_ref, t_scr, v_scr, r_scr):
    read_rows(in_ref, t_scr, 1)
    r_scr[...] = jnp.zeros(r_scr.shape, F32)
    for g in range(KG):
        blocks = [
            t_scr[:, SLOTS * g + q].astype(F32).reshape(CH, LANES) if SLOTS * g + q < KB else None
            for q in range(SLOTS)
        ]
        for s, value in enumerate(swap_slots(blocks)):
            v_scr[s] = value
            for b in range(NB):
                to = LANES * (b // SLOTS) + SLOT * (b % SLOTS) + GROUPS * s
                r_scr[to : to + GROUPS, part_lanes(g)] = v_scr[s, ROWS * b : ROWS * b + GROUPS]
    right_ref[...] = r_scr[...].astype(BF)


def assemble_right(received):
    return pl.pallas_call(
        assemble_right_kernel,
        out_shape=jax.ShapeDtypeStruct((JG * LANES, KG * LANES), BF),
        scratch_shapes=[
            pltpu.VMEM((NB, KB, ROWS, LANES), BF),
            pltpu.VMEM((SLOTS, CH, LANES), F32),
            pltpu.VMEM((JG * LANES, KG * LANES), F32),
        ],
        compiler_params=params(),
        cost_estimate=pl.CostEstimate(flops=2_000_000, bytes_accessed=1_000_000, transcendentals=0),
        name="assemble_right",
    )(received.reshape(NB, KB, PART, 2 * PARTS * LANES))


def product_messages(left_ref, right_ref, out_ref, place, t_scr):
    prod = dot(left_ref[...], right_ref[...], 1, 1)
    for g in range(JG):
        blocks = [prod[CH * s : CH * (s + 1), part_lanes(g)] for s in range(SLOTS)]
        for q, value in enumerate(swap_slots(blocks)):
            b = SLOTS * g + q
            if b < NB:
                write_rows(out_ref, place(b), value, t_scr)


def products_own_kernel(left_ref, right_ref, out_ref, t_scr):
    product_messages(left_ref, right_ref, out_ref, lambda b: b, t_scr)


def products_own(left, right):
    return pl.pallas_call(
        products_own_kernel,
        out_shape=message((NB, NB)),
        scratch_shapes=[pltpu.VMEM((NB, ROWS, LANES), BF)],
        compiler_params=params(),
        cost_estimate=pl.CostEstimate(flops=230_000_000, bytes_accessed=1_400_000, transcendentals=0),
        name="products_own",
    )(left, right)


def products_kernel(core_ref, left_ref, right_ref, own_ref, out_ref, t_scr):
    core = core_ref[0]
    for b in range(NB):
        out_ref[:, 2 * b + core] = own_ref[:, b]
    product_messages(left_ref, right_ref, out_ref, lambda b: 2 * b + 1 - core, t_scr)


def products(core, left, other, own):
    return pl.pallas_call(
        products_kernel,
        out_shape=message((NB, KB)),
        in_specs=[pl.BlockSpec(memory_space=pltpu.SMEM)] + [pl.BlockSpec(memory_space=pltpu.VMEM)] * 3,
        scratch_shapes=[pltpu.VMEM((NB, ROWS, LANES), BF)],
        compiler_params=params(),
        cost_estimate=pl.CostEstimate(flops=230_000_000, bytes_accessed=1_600_000, transcendentals=0),
        name="products",
    )(core, left, other, own).reshape(CH, PART, PARTS * LANES)


def middle_kernel(
    prod_ref, gate_ref, slope_ref, dx_ref, cols_ref, w_ref,
    update_ref, out_ref, dgate_ref, p_scr, o_scr,
):
    unpack(prod_ref, p_scr)
    used = used_lanes((CH, LANES))
    gain, bias = cols_ref[:, 1:2], cols_ref[:, 2:3]
    for r in range(GROUPS):
        xhat, scale = normalized(by_row(p_scr)[row_at(r), :], 0)
        prodn = (xhat * gain + bias).astype(BF)
        mixed = dot(w_ref[...], prodn, 1, 0)
        gather_tile((gate_ref[r] * mixed).T, update_ref, r)
        dgate_ref[r] = (slope_ref[r] * mixed).astype(BF)
        d_prod = norm_grad(dx_ref[r], xhat, scale, 0)
        by_row(o_scr)[row_at(r), :] = jnp.where(used, d_prod, 0.0)
    pack(out_ref, o_scr)


def middle(prod, gate, slope, dx, cols, w_out_t):
    return pl.pallas_call(
        middle_kernel,
        out_shape=[
            pltpu.VMEM((TILE, TILE, CH), BF),
            message((CH,)),
            jax.ShapeDtypeStruct((GROUPS, CH, LANES), BF),
        ],
        scratch_shapes=[PADDED, PADDED],
        compiler_params=params(),
        cost_estimate=pl.CostEstimate(flops=50_000_000, bytes_accessed=4_000_000, transcendentals=10_000),
        name="middle",
    )(prod, gate, slope, dx, cols, w_out_t)


def regroup_kernel(core_ref, in_ref, keep_ref, send_ref, t_scr):
    core = core_ref[0]
    read_rows(in_ref, t_scr)
    for t, to_ref in enumerate((send_ref, keep_ref)):
        parity = 1 - core if t == 0 else core
        for g in range(JG):
            blocks = [
                t_scr[:, 2 * (SLOTS * g + q) + parity].astype(F32).reshape(CH, LANES) if SLOTS * g + q < NB else None
                for q in range(SLOTS)
            ]
            for s, value in enumerate(swap_slots(blocks)):
                to_ref[CH * s : CH * (s + 1), part_lanes(g)] = value.astype(BF)


def regroup(core, received):
    half = jax.ShapeDtypeStruct((SLOTS * NB * ROWS, JG * LANES), BF)
    return pl.pallas_call(
        regroup_kernel,
        out_shape=[half, half],
        in_specs=[pl.BlockSpec(memory_space=pltpu.SMEM), pl.BlockSpec(memory_space=pltpu.VMEM)],
        scratch_shapes=[pltpu.VMEM((NB, KB, ROWS, LANES), BF)],
        compiler_params=params(),
        cost_estimate=pl.CostEstimate(flops=2_000_000, bytes_accessed=1_000_000, transcendentals=0),
        name="regroup",
    )(core, received.reshape(NB, KB, PART, PARTS * LANES))


def left_grad_kernel(keep_ref, send_ref, own_ref, other_ref, left_hbm, out_ref, left_ref, t_scr, sems):
    rows = [pl.ds(CH * s, CH) for s in range(SLOTS)]
    copies = fetch([left_hbm.at[at] for at in rows], [left_ref.at[at] for at in rows], sems)
    for g in range(KG):
        lanes = part_lanes(g)
        d_left = dot(keep_ref[...], own_ref[:, lanes], 1, 0) + dot(send_ref[...], other_ref[:, lanes], 1, 0)
        for q, value in enumerate(swap_slots([d_left[CH * s : CH * (s + 1)] for s in range(SLOTS)])):
            if SLOTS * g + q < KB:
                write_rows(out_ref, SLOTS * g + q, value, t_scr)
    for copy in copies:
        copy.wait()


def left_grad(keep, send, own, other, left_other):
    return pl.pallas_call(
        left_grad_kernel,
        out_shape=[message((NB, KB)), jax.ShapeDtypeStruct((SLOTS * NB * ROWS, KG * LANES), BF)],
        in_specs=[pl.BlockSpec(memory_space=pltpu.VMEM)] * 4 + in_hbm(1),
        scratch_shapes=[pltpu.VMEM((NB, ROWS, LANES), BF), pltpu.SemaphoreType.DMA((SLOTS,))],
        compiler_params=params(),
        cost_estimate=pl.CostEstimate(flops=450_000_000, bytes_accessed=2_200_000, transcendentals=0),
        name="left_grad",
    )(keep, send, own, other, *keep_in_hbm(left_other))


def right_grad_kernel(
    keep_ref, other_ref, left_ref, left_other_ref, d_left_ref, update_ref, out_ref, update_hbm, d_scr, o_scr, sem
):
    copy = pltpu.make_async_copy(update_ref, update_hbm, sem)
    copy.start()
    out_ref[:, :, :, : PARTS * LANES] = d_left_ref[...]
    d_scr[...] = dot(keep_ref[...], left_ref[...], 0, 0) + dot(other_ref[...], left_other_ref[...], 0, 0)
    for g in range(KG):
        for b in range(NB):
            at = LANES * (b // SLOTS) + SLOT * (b % SLOTS)
            blocks = [d_scr[at + GROUPS * s : at + GROUPS * s + ROWS, part_lanes(g)] for s in range(SLOTS)]
            for q, value in enumerate(swap_slots(blocks)):
                if SLOTS * g + q < KB:
                    o_scr[b, SLOTS * g + q] = value.astype(o_scr.dtype)
    for p in range(PARTS):
        out_ref[:, :, :, part_lanes(PARTS + p)] = o_scr[:, :, PART * p : PART * (p + 1), :].astype(BF)
    copy.wait()


def right_grad(keep, other, left, left_other, d_left, update):
    out, update = pl.pallas_call(
        right_grad_kernel,
        out_shape=[message((NB, KB), 2), jax.ShapeDtypeStruct((TILE, TILE, CH), BF)],
        out_specs=[pl.BlockSpec(memory_space=pltpu.VMEM), pl.BlockSpec(memory_space=pltpu.HBM)],
        scratch_shapes=[
            pltpu.VMEM((JG * LANES, KG * LANES), F32),
            pltpu.VMEM((NB, KB, ROWS, LANES), BF),
            pltpu.SemaphoreType.DMA,
        ],
        compiler_params=params(),
        cost_estimate=pl.CostEstimate(flops=450_000_000, bytes_accessed=2_500_000, transcendentals=0),
        name="right_grad",
    )(keep, other, left, left_other, d_left, pltpu.with_memory_space_constraint(update, pltpu.VMEM))
    return out.reshape(CH, PART, 2 * PARTS * LANES), update


def finish_kernel(
    d_ref, fac_ref, dgate_ref, xhat_ref, scale_ref, cols_ref, w_ref, out_hbm, l_scr, r_scr, out_ref, sems
):
    copies = []
    unpack(d_ref, l_scr, 0)
    unpack(d_ref, r_scr, 1)
    gain = cols_ref[:, 0:1]
    for r in range(GROUPS):
        d_left = by_row(l_scr)[row_at(r), :]
        d_right = by_row(r_scr)[row_at(r), :]
        parts = [
            (d * fac_ref[r, CH * f : CH * (f + 1), :].astype(F32)).astype(BF)
            for f, d in enumerate((d_left, d_left, d_right, d_right))
        ]
        d_proj = jnp.concatenate(parts + [dgate_ref[r]], 0)
        d_normed = dot(w_ref[...], d_proj, 1, 0).astype(BF).astype(F32)
        gather_tile(norm_grad(d_normed * gain, xhat_ref[r], scale_ref[r : r + 1, :], 0).T, out_ref, r)
        copies += send_tile(out_ref, out_hbm, r, sems)
    for copy in copies:
        copy.wait()


def finish(d_edges, fac, dgate, xhat, scale, cols, w_in):
    return pl.pallas_call(
        finish_kernel,
        out_shape=jax.ShapeDtypeStruct((TILE, TILE, CH), BF),
        out_specs=pl.BlockSpec(memory_space=pltpu.HBM),
        scratch_shapes=[
            PADDED,
            PADDED,
            pltpu.VMEM((TILE, TILE, CH), BF),
            pltpu.SemaphoreType.DMA((TILE // PART,)),
        ],
        compiler_params=params(),
        cost_estimate=pl.CostEstimate(flops=250_000_000, bytes_accessed=4_000_000, transcendentals=0),
        name="finish",
    )(d_edges, fac, dgate, xhat, scale, cols, w_in)


def exchange(x):
    return lax.all_to_all(x, WIDE, 0, 0, tiled=True)


def other_core(x):
    return lax.ppermute(x, "core", [(0, 1), (1, 0)])


def shards(pair, cotangent, gain_in, bias_in, w_in, gain_out, bias_out, w_out):
    gain_in, bias_in = gain_in.reshape(1, CH), bias_in.reshape(1, CH)
    gain_out, bias_out = gain_out.reshape(1, CH), bias_out.reshape(1, CH)
    core = lax.axis_index("core").astype(jnp.int32).reshape(1)
    received = exchange(edges(pair, w_in, gain_in, bias_in))
    ready = side(pair, cotangent, w_in, w_out, gain_in, bias_in, gain_out, bias_out)
    received, ready = lax.optimization_barrier((received, ready))
    gate, slope, dx, fac, xhat, scale, cols, w_in, w_out_t = ready
    right = assemble_right(received)
    right_other = other_core(right)
    left = assemble_left(received)
    left_other = other_core(left)
    prod = products(core, left, right_other, products_own(left, right))
    prod, left_other = lax.optimization_barrier((prod, left_other))
    update, d_prod, dgate = middle(exchange(prod), gate, slope, dx, cols, w_out_t)
    keep, send = regroup(core, exchange(d_prod))
    sent = other_core(send)
    d_left, left_other = left_grad(keep, send, right, right_other, left_other)
    d_edges, update = right_grad(keep, sent, left, left_other, d_left, update)
    d_edges = exchange(d_edges)
    grad = finish(d_edges, fac, dgate, xhat, scale, cols, w_in)
    return update, grad


def solution(mesh):
    split = Mesh(mesh.devices.reshape(2, 4, 2, 4, 4), NAMES)
    tile = P(("zh", "x", "core"), ("y", "zl"), None)
    return jax.shard_map(
        shards,
        mesh=split,
        in_specs=(tile, tile, P(), P(), P(), P(), P(), P()),
        out_specs=(tile, tile),
        check_vma=False,
    )
```

profile of v0, /device:TPU:1, one launch (start us, length us, event | category | flops | bytes accessed | tf_op | source)
XLA Modules:
  0.0 137.2 jit_solution(2596914681081163575)
XLA Ops:
  0.6 3.1 %edges.1 = bf16[128,4,768]{2,1,0:T(4,128)(2,1)} custom-call(bf16[36,36,128]{2,1,0:T(8,128)(2,1)} %pair_hbm.3, bf16[128,640]{1,0:T(8,128)(2,1)} %w_hbm.3, f32[1,128]{1,0:T(1,128)} %bitcast.14, f32[1,128]{1,0:T(1,128)} %bitcast.16), custom_call_target="tpu_custom_call" | custom-call | flops 200000000 | bytes 1200000 | tf_op jit(solution)/shard_map/edges/pallas_call | solution.py:190
  3.8 16.4 %all-to-all-start = ((bf16[128,4,768]{2,1,0:T(4,128)(2,1)}), bf16[128,4,768]{2,1,0:T(4,128)(2,1)S(1)}, u32[]{:S(2)}, u32[]{:S(2)}) async-start(bf16[128,4,768]{2,1,0:T(4,128)(2,1)} %edges.1), calls=%async_computation | async-start | bytes 1572864 | tf_op jit(solution)/shard_map/all_to_all | solution.py:546
  20.1 4.4 %side.1 = (f32[12,128,128]{2,1,0:T(8,128)S(1)}, f32[12,128,128]{2,1,0:T(8,128)S(1)}, f32[12,128,128]{2,1,0:T(8,128)S(1)}, bf16[12,512,128]{2,1,0:T(8,128)(2,1)S(...) custom-call(bf16[36,36,128]{2,1,0:T(8,128)(2,1)} %pair_hbm.3, ...), custom_call_target="tpu_custom_call" | custom-call | flops 300000000 | bytes 6000000 | tf_op jit(solution)/shard_map/side/pallas_call | solution.py:258
  24.5 1.2 copy-done
  25.7 0.9 copy-done.2
  26.6 0.9 copy-done.4
  27.5 0.9 copy-done.6
  28.4 0.7 copy-done.8
  29.0 16.1 %all-to-all-done = bf16[128,4,768]{2,1,0:T(4,128)(2,1)S(1)} async-done(((bf16[128,4,768]{2,1,0:T(4,128)(2,1)}), bf16[128,4,768]{2,1,0:T(4,128)(2,1)S(1)}, u32[]{:S(2)}, u32[]{:S(2)}) %all-to-all-start) | async-done | bytes 786464 | tf_op jit(solution)/shard_map/all_to_all | solution.py:546
  45.2 0.6 assemble_right.1.right_ref.own_ref
  45.8 2.1 %collective-permute-start = (bf16[384,768]{1,0:T(8,128)(2,1)S(1)}, bf16[384,768]{1,0:T(8,128)(2,1)S(1)}, u32[]{:S(2)}, u32[]{:S(2)}) collective-permute-start(bf16[384,768]{1,0:T(8,128)(2,1)S(1)} %assemble_right.1.right_ref.own_ref), channel_id=1, source_target_pairs={{0,16},{16,0},{1,17},{17,1},{2,18},{18,2},{3,19},{19,3},{4,20},{20... | collective-permute-start | bytes 1769480 | tf_op jit(solution)/shard_map/ppermute | solution.py:550
  47.9 0.5 assemble_left.1.left_ref
  48.5 0.7 products_own.1.own_ref
  49.2 0.4 collective-permute-done.right_ref.other_ref
  49.6 0.7 products.1
  50.6 22.6 %all_to_all.20.prod_ref = bf16[128,4,384]{2,1,0:T(4,128)(2,1)S(1)} all-to-all(bf16[128,4,384]{2,1,0:T(4,128)(2,1)S(1)} %bitcast.12), channel_id=1, replica_groups=mesh['zh'=2,'x'=4,'core'=2,'y'=4,'zl'=4] {'zh','x','y','zl'}, dimensions={0} | all-to-all | bytes 786432 | tf_op jit(solution)/shard_map/all_to_all | solution.py:546
  73.2 1.2 middle.1
  74.5 22.4 %all_to_all.21 = bf16[128,4,384]{2,1,0:T(4,128)(2,1)S(1)} all-to-all(bf16[128,4,384]{2,1,0:T(4,128)(2,1)S(1)} %get-tuple-element.48), channel_id=1, replica_groups=mesh['zh'=2,'x'=4,'core'=2,'y'=4,'zl'=4] {'zh','x','y','zl'}, dimensions={0} | all-to-all | bytes 786432 | tf_op jit(solution)/shard_map/all_to_all | solution.py:546
  96.8 0.5 regroup.1
  97.4 2.4 %collective-permute-start.2 = (bf16[384,384]{1,0:T(8,128)(2,1)S(1)}, bf16[384,384]{1,0:T(8,128)(2,1)S(1)}, u32[]{:S(2)}, u32[]{:S(2)}) collective-permute-start(bf16[384,384]{1,0:T(8,128)(2,1)S(1)} %get-tuple-element.50.send_ref), channel_id=1, source_target_pairs={{0,16},{16,0},{1,17},{17,1},{2,18},{18,2},{3,19},{19,3},{4,20},{20... | collective-permute-start | bytes 884744 | tf_op jit(solution)/shard_map/ppermute | solution.py:550
  99.8 2.1 %left_grad.1 = (bf16[8,16,4,384]{3,2,1,0:T(4,128)(2,1)S(1)}, bf16[384,768]{1,0:T(8,128)(2,1)S(1)}) custom-call(bf16[384,384]{1,0:T(8,128)(2,1)S(1)} %get-tuple-element.49.keep_ref, bf16[384,384]{1,0:T(8,128)(2,1)S(1)} %get-tuple-element.50.send_ref, bf16[384,768]{1,0:T(8,128)(2,1)S(1)} %assemble_right.1.right_ref.own_ref, ...), custom_call_target="tpu_custom_call" | custom-call | flops 450000000 | bytes 2200000 | tf_op jit(solution)/shard_map/left_grad/pallas_call | solution.py:459
  102.0 1.2 right_grad.1
  103.1 31.8 %all_to_all.22.d_ref = bf16[128,4,768]{2,1,0:T(4,128)(2,1)S(1)} all-to-all(bf16[128,4,768]{2,1,0:T(4,128)(2,1)S(1)} %bitcast.13), channel_id=1, replica_groups=mesh['zh'=2,'x'=4,'core'=2,'y'=4,'zl'=4] {'zh','x','y','zl'}, dimensions={0} | all-to-all | bytes 1572864 | tf_op jit(solution)/shard_map/all_to_all | solution.py:546
  134.9 2.1 %finish.1 = bf16[36,36,128]{2,1,0:T(8,128)(2,1)} custom-call(bf16[128,4,768]{2,1,0:T(4,128)(2,1)S(1)} %all_to_all.22.d_ref, bf16[12,512,128]{2,1,0:T(8,128)(2,1)S(1)} %copy-done.1, bf16[12,128,128]{2,1,0:T(8,128)(2,1)S(1)} %get-tuple-element.58.dgate_ref, f32[12,128,128]{2,1,0:T(8,128)S(1)} %copy-done.7, f32[16,128]{1,0:T(8,128)S(1)} %get-tuple-element.60.scale_ref, ...), custom_call_target="tpu_custom_call" | custom-call | flops 250000000 | bytes 4000000 | tf_op jit(solution)/shard_map/finish/pallas_call | solution.py:529
  (18 shorter events, 0.5 us)
Async XLA Ops:
  3.8 41.4 %all-to-all-start = ((bf16[128,4,768]{2,1,0:T(4,128)(2,1)}), bf16[128,4,768]{2,1,0:T(4,128)(2,1)S(1)}, u32[]{:S(2)}, u32[]{:S(2)}) async-start(bf16[128,4,768]{2,1,0:T(4,128)(2,1)} %edges.1), calls=%async_computation | async-start | bytes 1572864 | tf_op jit(solution)/shard_map/all_to_all | solution.py:546
  24.5 1.2 copy-start
  25.7 0.9 copy-start.2
  26.6 0.9 copy-start.4
  27.5 0.9 copy-start.6
  28.4 0.7 copy-start.8
  45.8 3.8 %collective-permute-start = (bf16[384,768]{1,0:T(8,128)(2,1)S(1)}, bf16[384,768]{1,0:T(8,128)(2,1)S(1)}, u32[]{:S(2)}, u32[]{:S(2)}) collective-permute-start(bf16[384,768]{1,0:T(8,128)(2,1)S(1)} %assemble_right.1.right_ref.own_ref), channel_id=1, source_target_pairs={{0,16},{16,0},{1,17},{17,1},{2,18},{18,2},{3,19},{19,3},{4,20},{20... | collective-permute-start | bytes 1769480 | tf_op jit(solution)/shard_map/ppermute | solution.py:550
  48.4 2.2 %collective-permute-start.1 = (bf16[384,768]{1,0:T(8,128)(2,1)S(1)}, bf16[384,768]{1,0:T(8,128)(2,1)}, u32[]{:S(2)}, u32[]{:S(2)}) collective-permute-start(bf16[384,768]{1,0:T(8,128)(2,1)S(1)} %assemble_left.1.left_ref), channel_id=1, source_target_pairs={{0,16},{16,0},{1,17},{17,1},{2,18},{18,2},{3,19},{19,3},{4,20},{20... | collective-permute-start | bytes 1769480 | tf_op jit(solution)/shard_map/ppermute | solution.py:550
  49.2 24.0 %copy-start.3 = (f32[12,128,128]{2,1,0:T(8,128)S(1)}, f32[12,128,128]{2,1,0:T(8,128)}, u32[]{:S(2)}) copy-start(f32[12,128,128]{2,1,0:T(8,128)} %copy-done.2) | copy-start | bytes 2359300
  49.2 24.0 %copy-start.5 = (f32[12,128,128]{2,1,0:T(8,128)S(1)}, f32[12,128,128]{2,1,0:T(8,128)}, u32[]{:S(2)}) copy-start(f32[12,128,128]{2,1,0:T(8,128)} %copy-done.4) | copy-start | bytes 2359300
  97.4 4.5 %collective-permute-start.2 = (bf16[384,384]{1,0:T(8,128)(2,1)S(1)}, bf16[384,384]{1,0:T(8,128)(2,1)S(1)}, u32[]{:S(2)}, u32[]{:S(2)}) collective-permute-start(bf16[384,384]{1,0:T(8,128)(2,1)S(1)} %get-tuple-element.50.send_ref), channel_id=1, source_target_pairs={{0,16},{16,0},{1,17},{17,1},{2,18},{18,2},{3,19},{19,3},{4,20},{20... | collective-permute-start | bytes 884744 | tf_op jit(solution)/shard_map/ppermute | solution.py:550
  101.9 33.0 %copy-start.1 = (bf16[12,512,128]{2,1,0:T(8,128)(2,1)S(1)}, bf16[12,512,128]{2,1,0:T(8,128)(2,1)}, u32[]{:S(2)}) copy-start(bf16[12,512,128]{2,1,0:T(8,128)(2,1)} %copy-done) | copy-start | bytes 4718596
  102.0 32.9 %copy-start.7 = (f32[12,128,128]{2,1,0:T(8,128)S(1)}, f32[12,128,128]{2,1,0:T(8,128)}, u32[]{:S(2)}) copy-start(f32[12,128,128]{2,1,0:T(8,128)} %copy-done.6) | copy-start | bytes 2359300
  102.0 32.9 %copy-start.9 = (bf16[128,640]{1,0:T(8,128)(2,1)S(1)}, bf16[128,640]{1,0:T(8,128)(2,1)}, u32[]{:S(2)}) copy-start(bf16[128,640]{1,0:T(8,128)(2,1)} %copy-done.8) | copy-start | bytes 491524
where the time goes:
time: 137 us
  blocking collectives  76.7 us (56%)
  starting transfers between devices  21.1 us (15%)
  Pallas kernels  17.1 us (12%)
  waiting for transfers between devices  16.9 us (12%)
  local copies, waits for them, and re-layouts  4.52 us (3%)
    all_to_all x3, blocking collectives, exchange(): return lax.all_to_all(x, WIDE, 0, 0, tiled=True)  76.7 us
    all_to_all x1, starting transfers between devices, exchange(): return lax.all_to_all(x, WIDE, 0, 0, tiled=True)  16.4 us
    all_to_all x1, waiting for transfers between devices, exchange(): return lax.all_to_all(x, WIDE, 0, 0, tiled=True)  16.1 us
    ppermute x3, starting transfers between devices, other_core(): return lax.ppermute(x, 'core', [(0, 1), (1, 0)])  4.7 us
    unnamed x20, local copies, waits for them, and re-layouts  4.52 us
    pallas_call x1, Pallas kernels, side(): pl.pallas_call(side_kernel, out_shape=[square, square, square, jax.ShapeD...  4.39 us
    pallas_call x1, Pallas kernels, edges(): pl.pallas_call(edges_kernel, out_shape=message((CH,), 2), in_specs=in_hbm...  3.15 us
  transfers between devices with their start and end apart: 4, of which 3 were waited for; matrix products, arithmetic and copies ran while one was open for 0% of the time, Pallas kernels for 6%

commit v1 on v0

--- a/solution.py
+++ b/solution.py
@@ -24,7 +24,8 @@
 JG = 3
 CHUNKS = 4
 NAMES = ("zh", "x", "core", "y", "zl")
-WIDE = ("zh", "x", "y", "zl")
+WIDE = ("zh", "zl", "x", "y")
+BLOCKS = (2, 4, 4, 4)
 
 
 def params(mib=14):
@@ -121,15 +122,28 @@
 
 
 def read_rows(in_ref, scr, array=0):
-    scr[:, :, GROUPS:, :] = jnp.zeros((NB, KB, ROWS - GROUPS, LANES), scr.dtype)
+    scr[:, :, :, :, GROUPS:, :] = jnp.zeros(BLOCKS + (ROWS - GROUPS, LANES), scr.dtype)
     for p in range(PARTS):
-        scr[:, :, PART * p : PART * (p + 1), :] = in_ref[:, :, :, part_lanes(array * PARTS + p)].astype(scr.dtype)
+        part = in_ref[:, :, :, :, :, part_lanes(array * PARTS + p)]
+        scr[:, :, :, :, PART * p : PART * (p + 1), :] = part.astype(scr.dtype)
 
 
 def write_rows(out_ref, at, value, scr):
     scr[...] = value.astype(scr.dtype).reshape(NB, ROWS, LANES)
     for p in range(PARTS):
-        out_ref[:, at, :, part_lanes(p)] = scr[:, PART * p : PART * (p + 1), :].astype(BF)
+        part = scr[:, PART * p : PART * (p + 1), :].astype(BF)
+        if isinstance(at, tuple):
+            out_ref[(*at, slice(None), part_lanes(p))] = by_block(part)
+        else:
+            out_ref[:, at, :, part_lanes(p)] = part
+
+
+def column_block(k, parity=0):
+    return (slice(None), k % 4 + parity, slice(None), k // 4)
+
+
+def by_block(value):
+    return value.reshape(BLOCKS[0], BLOCKS[2], *value.shape[1:])
 
 
 def column(row):
@@ -289,7 +303,7 @@
     read_rows(in_ref, t_scr)
     for g in range(KG):
         blocks = [
-            t_scr[:, SLOTS * g + q].astype(F32).reshape(CH, LANES) if SLOTS * g + q < KB else None
+            t_scr[column_block(SLOTS * g + q)].astype(F32).reshape(CH, LANES) if SLOTS * g + q < KB else None
             for q in range(SLOTS)
         ]
         for s, value in enumerate(swap_slots(blocks)):
@@ -300,11 +314,11 @@
     return pl.pallas_call(
         assemble_left_kernel,
         out_shape=jax.ShapeDtypeStruct((SLOTS * NB * ROWS, KG * LANES), BF),
-        scratch_shapes=[pltpu.VMEM((NB, KB, ROWS, LANES), BF)],
+        scratch_shapes=[pltpu.VMEM(BLOCKS + (ROWS, LANES), BF)],
         compiler_params=params(),
         cost_estimate=pl.CostEstimate(flops=2_000_000, bytes_accessed=1_000_000, transcendentals=0),
         name="assemble_left",
-    )(received.reshape(NB, KB, PART, 2 * PARTS * LANES))
+    )(received.reshape(BLOCKS + (PART, 2 * PARTS * LANES)))
 
 
 def assemble_right_kernel(in_ref, right_ref, t_scr, v_scr, r_scr):
@@ -312,7 +326,7 @@
     r_scr[...] = jnp.zeros(r_scr.shape, F32)
     for g in range(KG):
         blocks = [
-            t_scr[:, SLOTS * g + q].astype(F32).reshape(CH, LANES) if SLOTS * g + q < KB else None
+            t_scr[column_block(SLOTS * g + q)].astype(F32).reshape(CH, LANES) if SLOTS * g + q < KB else None
             for q in range(SLOTS)
         ]
         for s, value in enumerate(swap_slots(blocks)):
@@ -328,14 +342,14 @@
         assemble_right_kernel,
         out_shape=jax.ShapeDtypeStruct((JG * LANES, KG * LANES), BF),
         scratch_shapes=[
-            pltpu.VMEM((NB, KB, ROWS, LANES), BF),
+            pltpu.VMEM(BLOCKS + (ROWS, LANES), BF),
             pltpu.VMEM((SLOTS, CH, LANES), F32),
             pltpu.VMEM((JG * LANES, KG * LANES), F32),
         ],
         compiler_params=params(),
         cost_estimate=pl.CostEstimate(flops=2_000_000, bytes_accessed=1_000_000, transcendentals=0),
         name="assemble_right",
-    )(received.reshape(NB, KB, PART, 2 * PARTS * LANES))
+    )(received.reshape(BLOCKS + (PART, 2 * PARTS * LANES)))
 
 
 def product_messages(left_ref, right_ref, out_ref, place, t_scr):
@@ -366,14 +380,14 @@
 def products_kernel(core_ref, left_ref, right_ref, own_ref, out_ref, t_scr):
     core = core_ref[0]
     for b in range(NB):
-        out_ref[:, 2 * b + core] = own_ref[:, b]
-    product_messages(left_ref, right_ref, out_ref, lambda b: 2 * b + 1 - core, t_scr)
+        out_ref[column_block(2 * b, core)] = by_block(own_ref[:, b])
+    product_messages(left_ref, right_ref, out_ref, lambda b: column_block(2 * b, 1 - core), t_scr)
 
 
 def products(core, left, other, own):
     return pl.pallas_call(
         products_kernel,
-        out_shape=message((NB, KB)),
+        out_shape=message(BLOCKS),
         in_specs=[pl.BlockSpec(memory_space=pltpu.SMEM)] + [pl.BlockSpec(memory_space=pltpu.VMEM)] * 3,
         scratch_shapes=[pltpu.VMEM((NB, ROWS, LANES), BF)],
         compiler_params=params(),
@@ -422,7 +436,9 @@
         parity = 1 - core if t == 0 else core
         for g in range(JG):
             blocks = [
-                t_scr[:, 2 * (SLOTS * g + q) + parity].astype(F32).reshape(CH, LANES) if SLOTS * g + q < NB else None
+                t_scr[column_block(2 * (SLOTS * g + q), parity)].astype(F32).reshape(CH, LANES)
+                if SLOTS * g + q < NB
+                else None
                 for q in range(SLOTS)
             ]
             for s, value in enumerate(swap_slots(blocks)):
@@ -435,11 +451,11 @@
         regroup_kernel,
         out_shape=[half, half],
         in_specs=[pl.BlockSpec(memory_space=pltpu.SMEM), pl.BlockSpec(memory_space=pltpu.VMEM)],
-        scratch_shapes=[pltpu.VMEM((NB, KB, ROWS, LANES), BF)],
+        scratch_shapes=[pltpu.VMEM(BLOCKS + (ROWS, LANES), BF)],
         compiler_params=params(),
         cost_estimate=pl.CostEstimate(flops=2_000_000, bytes_accessed=1_000_000, transcendentals=0),
         name="regroup",
-    )(core, received.reshape(NB, KB, PART, PARTS * LANES))
+    )(core, received.reshape(BLOCKS + (PART, PARTS * LANES)))
 
 
 def left_grad_kernel(keep_ref, send_ref, own_ref, other_ref, left_hbm, out_ref, left_ref, t_scr, sems):
@@ -450,7 +466,7 @@
         d_left = dot(keep_ref[...], own_ref[:, lanes], 1, 0) + dot(send_ref[...], other_ref[:, lanes], 1, 0)
         for q, value in enumerate(swap_slots([d_left[CH * s : CH * (s + 1)] for s in range(SLOTS)])):
             if SLOTS * g + q < KB:
-                write_rows(out_ref, SLOTS * g + q, value, t_scr)
+                write_rows(out_ref, column_block(SLOTS * g + q), value, t_scr)
     for copy in copies:
         copy.wait()
 
@@ -458,7 +474,7 @@
 def left_grad(keep, send, own, other, left_other):
     return pl.pallas_call(
         left_grad_kernel,
-        out_shape=[message((NB, KB)), jax.ShapeDtypeStruct((SLOTS * NB * ROWS, KG * LANES), BF)],
+        out_shape=[message(BLOCKS), jax.ShapeDtypeStruct((SLOTS * NB * ROWS, KG * LANES), BF)],
         in_specs=[pl.BlockSpec(memory_space=pltpu.VMEM)] * 4 + in_hbm(1),
         scratch_shapes=[pltpu.VMEM((NB, ROWS, LANES), BF), pltpu.SemaphoreType.DMA((SLOTS,))],
         compiler_params=params(),
@@ -472,7 +488,7 @@
 ):
     copy = pltpu.make_async_copy(update_ref, update_hbm, sem)
     copy.start()
-    out_ref[:, :, :, : PARTS * LANES] = d_left_ref[...]
+    out_ref[:, :, :, :, :, : PARTS * LANES] = d_left_ref[...]
     d_scr[...] = dot(keep_ref[...], left_ref[...], 0, 0) + dot(other_ref[...], left_other_ref[...], 0, 0)
     for g in range(KG):
         for b in range(NB):
@@ -480,20 +496,21 @@
             blocks = [d_scr[at + GROUPS * s : at + GROUPS * s + ROWS, part_lanes(g)] for s in range(SLOTS)]
             for q, value in enumerate(swap_slots(blocks)):
                 if SLOTS * g + q < KB:
-                    o_scr[b, SLOTS * g + q] = value.astype(o_scr.dtype)
+                    k = SLOTS * g + q
+                    o_scr[b // 4, k % 4, b % 4, k // 4] = value.astype(o_scr.dtype)
     for p in range(PARTS):
-        out_ref[:, :, :, part_lanes(PARTS + p)] = o_scr[:, :, PART * p : PART * (p + 1), :].astype(BF)
+        out_ref[:, :, :, :, :, part_lanes(PARTS + p)] = o_scr[:, :, :, :, PART * p : PART * (p + 1), :].astype(BF)
     copy.wait()
 
 
 def right_grad(keep, other, left, left_other, d_left, update):
     out, update = pl.pallas_call(
         right_grad_kernel,
-        out_shape=[message((NB, KB), 2), jax.ShapeDtypeStruct((TILE, TILE, CH), BF)],
+        out_shape=[message(BLOCKS, 2), jax.ShapeDtypeStruct((TILE, TILE, CH), BF)],
         out_specs=[pl.BlockSpec(memory_space=pltpu.VMEM), pl.BlockSpec(memory_space=pltpu.HBM)],
         scratch_shapes=[
             pltpu.VMEM((JG * LANES, KG * LANES), F32),
-            pltpu.VMEM((NB, KB, ROWS, LANES), BF),
+            pltpu.VMEM(BLOCKS + (ROWS, LANES), BF),
             pltpu.SemaphoreType.DMA,
         ],
         compiler_params=params(),

time: 137 us -> 136 us (level)
  blocking collectives: 76.7 us -> 73.6 us
  starting transfers between devices: 21.1 us -> 23.9 us
  waiting for transfers between devices: 16.9 us -> 15.4 us
    all_to_all x3, blocking collectives: 76.7 us -> 73.6 us  [exchange(): return lax.all_to_all(x, WIDE, 0, 0, tiled=True)]
    ppermute x3, starting transfers between devices: 4.7 us -> 7.53 us  [other_core(): return lax.ppermute(x, 'core', [(0, 1), (1, 0)])]
    all_to_all x1, waiting for transfers between devices: 16.1 us -> 14.7 us  [exchange(): return lax.all_to_all(x, WIDE, 0, 0, tiled=True)]
where the time goes in v1:
time: 136 us; the launch traced here: 135 us
  blocking collectives  73.6 us (54%)
  starting transfers between devices  23.9 us (18%)
  Pallas kernels  17.1 us (13%)
  waiting for transfers between devices  15.4 us (11%)
  local copies, waits for them, and re-layouts  4.52 us (3%)
    all_to_all x3, blocking collectives, exchange(): return lax.all_to_all(x, WIDE, 0, 0, tiled=True)  73.6 us
    all_to_all x1, starting transfers between devices, exchange(): return lax.all_to_all(x, WIDE, 0, 0, tiled=True)  16.4 us
    all_to_all x1, waiting for transfers between devices, exchange(): return lax.all_to_all(x, WIDE, 0, 0, tiled=True)  14.7 us
    ppermute x3, starting transfers between devices, other_core(): return lax.ppermute(x, 'core', [(0, 1), (1, 0)])  7.53 us
    unnamed x20, local copies, waits for them, and re-layouts  4.52 us
    pallas_call x1, Pallas kernels, side(): pl.pallas_call(side_kernel, out_shape=[square, square, square, jax.ShapeD...  4.39 us
    pallas_call x1, Pallas kernels, edges(): pl.pallas_call(edges_kernel, out_shape=message((CH,), 2), in_specs=in_hbm...  3.15 us
  transfers between devices with their start and end apart: 4, of which 3 were waited for; matrix products, arithmetic and copies ran while one was open for 0% of the time, Pallas kernels for 6%

profile of v1, /device:TPU:1, one launch (start us, length us, event | category | flops | bytes accessed | tf_op | source)
XLA Modules:
  0.0 135.4 jit_solution(14813357390599631882)
XLA Ops:
  0.6 3.1 %edges.1 = bf16[128,4,768]{2,1,0:T(4,128)(2,1)} custom-call(bf16[36,36,128]{2,1,0:T(8,128)(2,1)} %pair_hbm.3, bf16[128,640]{1,0:T(8,128)(2,1)} %w_hbm.3, f32[1,128]{1,0:T(1,128)} %bitcast.14, f32[1,128]{1,0:T(1,128)} %bitcast.16), custom_call_target="tpu_custom_call" | custom-call | flops 200000000 | bytes 1200000 | tf_op jit(solution)/shard_map/edges/pallas_call | solution.py:204
  3.8 16.4 %all-to-all-start = ((bf16[128,4,768]{2,1,0:T(4,128)(2,1)}), bf16[128,4,768]{2,1,0:T(4,128)(2,1)S(1)}, u32[]{:S(2)}, u32[]{:S(2)}) async-start(bf16[128,4,768]{2,1,0:T(4,128)(2,1)} %edges.1), calls=%async_computation | async-start | bytes 1572864 | tf_op jit(solution)/shard_map/all_to_all | solution.py:563
  20.1 4.4 %side.1 = (f32[12,128,128]{2,1,0:T(8,128)S(1)}, f32[12,128,128]{2,1,0:T(8,128)S(1)}, f32[12,128,128]{2,1,0:T(8,128)S(1)}, bf16[12,512,128]{2,1,0:T(8,128)(2,1)S(...) custom-call(bf16[36,36,128]{2,1,0:T(8,128)(2,1)} %pair_hbm.3, ...), custom_call_target="tpu_custom_call" | custom-call | flops 300000000 | bytes 6000000 | tf_op jit(solution)/shard_map/side/pallas_call | solution.py:272
  24.5 1.2 copy-done
  25.7 0.9 copy-done.2
  26.6 0.9 copy-done.4
  27.5 0.9 copy-done.6
  28.4 0.7 copy-done.8
  29.0 14.7 %all-to-all-done = bf16[128,4,768]{2,1,0:T(4,128)(2,1)S(1)} async-done(((bf16[128,4,768]{2,1,0:T(4,128)(2,1)}), bf16[128,4,768]{2,1,0:T(4,128)(2,1)S(1)}, u32[]{:S(2)}, u32[]{:S(2)}) %all-to-all-start) | async-done | bytes 786464 | tf_op jit(solution)/shard_map/all_to_all | solution.py:563
  43.7 0.6 assemble_right.1.right_ref.own_ref
  44.3 3.6 %collective-permute-start = (bf16[384,768]{1,0:T(8,128)(2,1)S(1)}, bf16[384,768]{1,0:T(8,128)(2,1)S(1)}, u32[]{:S(2)}, u32[]{:S(2)}) collective-permute-start(bf16[384,768]{1,0:T(8,128)(2,1)S(1)} %assemble_right.1.right_ref.own_ref), channel_id=1, source_target_pairs={{0,16},{16,0},{1,17},{17,1},{2,18},{18,2},{3,19},{19,3},{4,20},{20... | collective-permute-start | bytes 1769480 | tf_op jit(solution)/shard_map/ppermute | solution.py:567
  47.9 0.5 assemble_left.1.left_ref
  48.5 0.7 products_own.1.own_ref
  49.2 0.4 collective-permute-done.right_ref.other_ref
  49.5 0.7 products.1
  50.6 22.1 %all_to_all.20.prod_ref = bf16[128,4,384]{2,1,0:T(4,128)(2,1)S(1)} all-to-all(bf16[128,4,384]{2,1,0:T(4,128)(2,1)S(1)} %bitcast.12), channel_id=1, replica_groups=mesh['zh'=2,'x'=4,'core'=2,'y'=4,'zl'=4] {'zh','zl','x','y'}, dimensions={0} | all-to-all | bytes 786432 | tf_op jit(solution)/shard_map/all_to_all | solution.py:563
  72.7 1.2 middle.1
  74.0 21.3 %all_to_all.21 = bf16[128,4,384]{2,1,0:T(4,128)(2,1)S(1)} all-to-all(bf16[128,4,384]{2,1,0:T(4,128)(2,1)S(1)} %get-tuple-element.48), channel_id=1, replica_groups=mesh['zh'=2,'x'=4,'core'=2,'y'=4,'zl'=4] {'zh','zl','x','y'}, dimensions={0} | all-to-all | bytes 786432 | tf_op jit(solution)/shard_map/all_to_all | solution.py:563
  95.2 0.5 regroup.1
  95.8 3.9 %collective-permute-start.2 = (bf16[384,384]{1,0:T(8,128)(2,1)S(1)}, bf16[384,384]{1,0:T(8,128)(2,1)S(1)}, u32[]{:S(2)}, u32[]{:S(2)}) collective-permute-start(bf16[384,384]{1,0:T(8,128)(2,1)S(1)} %get-tuple-element.50.send_ref), channel_id=1, source_target_pairs={{0,16},{16,0},{1,17},{17,1},{2,18},{18,2},{3,19},{19,3},{4,20},{20... | collective-permute-start | bytes 884744 | tf_op jit(solution)/shard_map/ppermute | solution.py:567
  99.6 2.1 %left_grad.1 = (bf16[2,4,4,4,4,384]{5,4,3,2,1,0:T(4,128)(2,1)S(1)}, bf16[384,768]{1,0:T(8,128)(2,1)S(1)}) custom-call(bf16[384,384]{1,0:T(8,128)(2,1)S(1)} %get-tuple-element.49.keep_ref, bf16[384,384]{1,0:T(8,128)(2,1)S(1)} %get-tuple-element.50.send_ref, bf16[384,768]{1,0:T(8,128)(2,1)S(1)} %assemble_right.1.right_ref.own_ref, ...), custom_call_target="tpu_custom_call" | custom-call | flops 450000000 | bytes 2200000 | tf_op jit(solution)/shard_map/left_grad/pallas_call | solution.py:475
  101.8 1.2 right_grad.1
  102.9 30.2 %all_to_all.22.d_ref = bf16[128,4,768]{2,1,0:T(4,128)(2,1)S(1)} all-to-all(bf16[128,4,768]{2,1,0:T(4,128)(2,1)S(1)} %bitcast.13), channel_id=1, replica_groups=mesh['zh'=2,'x'=4,'core'=2,'y'=4,'zl'=4] {'zh','zl','x','y'}, dimensions={0} | all-to-all | bytes 1572864 | tf_op jit(solution)/shard_map/all_to_all | solution.py:563
  133.2 2.1 %finish.1 = bf16[36,36,128]{2,1,0:T(8,128)(2,1)} custom-call(bf16[128,4,768]{2,1,0:T(4,128)(2,1)S(1)} %all_to_all.22.d_ref, bf16[12,512,128]{2,1,0:T(8,128)(2,1)S(1)} %copy-done.1, bf16[12,128,128]{2,1,0:T(8,128)(2,1)S(1)} %get-tuple-element.58.dgate_ref, f32[12,128,128]{2,1,0:T(8,128)S(1)} %copy-done.7, f32[16,128]{1,0:T(8,128)S(1)} %get-tuple-element.60.scale_ref, ...), custom_call_target="tpu_custom_call" | custom-call | flops 250000000 | bytes 4000000 | tf_op jit(solution)/shard_map/finish/pallas_call | solution.py:546
  (18 shorter events, 0.5 us)
Async XLA Ops:
  3.8 39.9 %all-to-all-start = ((bf16[128,4,768]{2,1,0:T(4,128)(2,1)}), bf16[128,4,768]{2,1,0:T(4,128)(2,1)S(1)}, u32[]{:S(2)}, u32[]{:S(2)}) async-start(bf16[128,4,768]{2,1,0:T(4,128)(2,1)} %edges.1), calls=%async_computation | async-start | bytes 1572864 | tf_op jit(solution)/shard_map/all_to_all | solution.py:563
  24.5 1.2 copy-start
  25.7 0.9 copy-start.2
  26.6 0.9 copy-start.4
  27.5 0.9 copy-start.6
  28.4 0.7 copy-start.8
  44.3 5.2 %collective-permute-start = (bf16[384,768]{1,0:T(8,128)(2,1)S(1)}, bf16[384,768]{1,0:T(8,128)(2,1)S(1)}, u32[]{:S(2)}, u32[]{:S(2)}) collective-permute-start(bf16[384,768]{1,0:T(8,128)(2,1)S(1)} %assemble_right.1.right_ref.own_ref), channel_id=1, source_target_pairs={{0,16},{16,0},{1,17},{17,1},{2,18},{18,2},{3,19},{19,3},{4,20},{20... | collective-permute-start | bytes 1769480 | tf_op jit(solution)/shard_map/ppermute | solution.py:567
  48.4 2.2 %collective-permute-start.1 = (bf16[384,768]{1,0:T(8,128)(2,1)S(1)}, bf16[384,768]{1,0:T(8,128)(2,1)}, u32[]{:S(2)}, u32[]{:S(2)}) collective-permute-start(bf16[384,768]{1,0:T(8,128)(2,1)S(1)} %assemble_left.1.left_ref), channel_id=1, source_target_pairs={{0,16},{16,0},{1,17},{17,1},{2,18},{18,2},{3,19},{19,3},{4,20},{20... | collective-permute-start | bytes 1769480 | tf_op jit(solution)/shard_map/ppermute | solution.py:567
  49.1 23.6 %copy-start.3 = (f32[12,128,128]{2,1,0:T(8,128)S(1)}, f32[12,128,128]{2,1,0:T(8,128)}, u32[]{:S(2)}) copy-start(f32[12,128,128]{2,1,0:T(8,128)} %copy-done.2) | copy-start | bytes 2359300
  49.1 23.6 %copy-start.5 = (f32[12,128,128]{2,1,0:T(8,128)S(1)}, f32[12,128,128]{2,1,0:T(8,128)}, u32[]{:S(2)}) copy-start(f32[12,128,128]{2,1,0:T(8,128)} %copy-done.4) | copy-start | bytes 2359300
  95.8 6.0 %collective-permute-start.2 = (bf16[384,384]{1,0:T(8,128)(2,1)S(1)}, bf16[384,384]{1,0:T(8,128)(2,1)S(1)}, u32[]{:S(2)}, u32[]{:S(2)}) collective-permute-start(bf16[384,384]{1,0:T(8,128)(2,1)S(1)} %get-tuple-element.50.send_ref), channel_id=1, source_target_pairs={{0,16},{16,0},{1,17},{17,1},{2,18},{18,2},{3,19},{19,3},{4,20},{20... | collective-permute-start | bytes 884744 | tf_op jit(solution)/shard_map/ppermute | solution.py:567
  101.7 31.4 %copy-start.1 = (bf16[12,512,128]{2,1,0:T(8,128)(2,1)S(1)}, bf16[12,512,128]{2,1,0:T(8,128)(2,1)}, u32[]{:S(2)}) copy-start(bf16[12,512,128]{2,1,0:T(8,128)(2,1)} %copy-done) | copy-start | bytes 4718596
  101.7 31.4 %copy-start.7 = (f32[12,128,128]{2,1,0:T(8,128)S(1)}, f32[12,128,128]{2,1,0:T(8,128)}, u32[]{:S(2)}) copy-start(f32[12,128,128]{2,1,0:T(8,128)} %copy-done.6) | copy-start | bytes 2359300
  101.8 31.4 %copy-start.9 = (bf16[128,640]{1,0:T(8,128)(2,1)S(1)}, bf16[128,640]{1,0:T(8,128)(2,1)}, u32[]{:S(2)}) copy-start(bf16[128,640]{1,0:T(8,128)(2,1)} %copy-done.8) | copy-start | bytes 491524

commit v2 on v1

--- a/solution.py
+++ b/solution.py
@@ -458,7 +458,9 @@
     )(core, received.reshape(BLOCKS + (PART, PARTS * LANES)))
 
 
-def left_grad_kernel(keep_ref, send_ref, own_ref, other_ref, left_hbm, out_ref, left_ref, t_scr, sems):
+def left_grad_kernel(
+    keep_ref, send_ref, own_ref, other_ref, left_own_ref, left_hbm, out_ref, left_ref, part_ref, t_scr, sems
+):
     rows = [pl.ds(CH * s, CH) for s in range(SLOTS)]
     copies = fetch([left_hbm.at[at] for at in rows], [left_ref.at[at] for at in rows], sems)
     for g in range(KG):
@@ -467,29 +469,32 @@
         for q, value in enumerate(swap_slots([d_left[CH * s : CH * (s + 1)] for s in range(SLOTS)])):
             if SLOTS * g + q < KB:
                 write_rows(out_ref, column_block(SLOTS * g + q), value, t_scr)
+    part_ref[...] = dot(keep_ref[...], left_own_ref[...], 0, 0)
     for copy in copies:
         copy.wait()
 
 
-def left_grad(keep, send, own, other, left_other):
+def left_grad(keep, send, own, other, left, left_other):
     return pl.pallas_call(
         left_grad_kernel,
-        out_shape=[message(BLOCKS), jax.ShapeDtypeStruct((SLOTS * NB * ROWS, KG * LANES), BF)],
-        in_specs=[pl.BlockSpec(memory_space=pltpu.VMEM)] * 4 + in_hbm(1),
+        out_shape=[message(BLOCKS), jax.ShapeDtypeStruct((SLOTS * NB * ROWS, KG * LANES), BF),
+            jax.ShapeDtypeStruct((JG * LANES, KG * LANES), F32),
+        ],
+        in_specs=[pl.BlockSpec(memory_space=pltpu.VMEM)] * 5 + in_hbm(1),
         scratch_shapes=[pltpu.VMEM((NB, ROWS, LANES), BF), pltpu.SemaphoreType.DMA((SLOTS,))],
         compiler_params=params(),
         cost_estimate=pl.CostEstimate(flops=450_000_000, bytes_accessed=2_200_000, transcendentals=0),
         name="left_grad",
-    )(keep, send, own, other, *keep_in_hbm(left_other))
+    )(keep, send, own, other, left, *keep_in_hbm(left_other))
 
 
 def right_grad_kernel(
-    keep_ref, other_ref, left_ref, left_other_ref, d_left_ref, update_ref, out_ref, update_hbm, d_scr, o_scr, sem
+    part_ref, other_ref, left_other_ref, d_left_ref, update_ref, out_ref, update_hbm, d_scr, o_scr, sem
 ):
     copy = pltpu.make_async_copy(update_ref, update_hbm, sem)
     copy.start()
     out_ref[:, :, :, :, :, : PARTS * LANES] = d_left_ref[...]
-    d_scr[...] = dot(keep_ref[...], left_ref[...], 0, 0) + dot(other_ref[...], left_other_ref[...], 0, 0)
+    d_scr[...] = part_ref[...] + dot(other_ref[...], left_other_ref[...], 0, 0)
     for g in range(KG):
         for b in range(NB):
             at = LANES * (b // SLOTS) + SLOT * (b % SLOTS)
@@ -503,7 +508,7 @@
     copy.wait()
 
 
-def right_grad(keep, other, left, left_other, d_left, update):
+def right_grad(part, other, left_other, d_left, update):
     out, update = pl.pallas_call(
         right_grad_kernel,
         out_shape=[message(BLOCKS, 2), jax.ShapeDtypeStruct((TILE, TILE, CH), BF)],
@@ -516,7 +521,7 @@
         compiler_params=params(),
         cost_estimate=pl.CostEstimate(flops=450_000_000, bytes_accessed=2_500_000, transcendentals=0),
         name="right_grad",
-    )(keep, other, left, left_other, d_left, pltpu.with_memory_space_constraint(update, pltpu.VMEM))
+    )(part, other, left_other, d_left, pltpu.with_memory_space_constraint(update, pltpu.VMEM))
     return out.reshape(CH, PART, 2 * PARTS * LANES), update
 
 
@@ -584,8 +589,8 @@
     update, d_prod, dgate = middle(exchange(prod), gate, slope, dx, cols, w_out_t)
     keep, send = regroup(core, exchange(d_prod))
     sent = other_core(send)
-    d_left, left_other = left_grad(keep, send, right, right_other, left_other)
-    d_edges, update = right_grad(keep, sent, left, left_other, d_left, update)
+    d_left, left_other, part = left_grad(keep, send, right, right_other, left, left_other)
+    d_edges, update = right_grad(part, sent, left_other, d_left, update)
     d_edges = exchange(d_edges)
     grad = finish(d_edges, fac, dgate, xhat, scale, cols, w_in)
     return update, grad

time: 136 us -> 136 us (level)
  no operation moved by 1% of the time
where the time goes in v2:
time: 136 us; the launch traced here: 135 us
  blocking collectives  73.6 us (54%)
  starting transfers between devices  23.9 us (18%)
  Pallas kernels  16.9 us (12%)
  waiting for transfers between devices  15.4 us (11%)
  local copies, waits for them, and re-layouts  4.52 us (3%)
    all_to_all x3, blocking collectives, exchange(): return lax.all_to_all(x, WIDE, 0, 0, tiled=True)  73.6 us
    all_to_all x1, starting transfers between devices, exchange(): return lax.all_to_all(x, WIDE, 0, 0, tiled=True)  16.4 us
    all_to_all x1, waiting for transfers between devices, exchange(): return lax.all_to_all(x, WIDE, 0, 0, tiled=True)  14.7 us
    ppermute x3, starting transfers between devices, other_core(): return lax.ppermute(x, 'core', [(0, 1), (1, 0)])  7.53 us
    unnamed x20, local copies, waits for them, and re-layouts  4.52 us
    pallas_call x1, Pallas kernels, side(): pl.pallas_call(side_kernel, out_shape=[square, square, square, jax.ShapeD...  4.39 us
    pallas_call x1, Pallas kernels, edges(): pl.pallas_call(edges_kernel, out_shape=message((CH,), 2), in_specs=in_hbm...  3.15 us
  transfers between devices with their start and end apart: 4, of which 3 were waited for; matrix products, arithmetic and copies ran while one was open for 0% of the time, Pallas kernels for 6%

profile of v2, /device:TPU:1, one launch (start us, length us, event | category | flops | bytes accessed | tf_op | source)
XLA Modules:
  0.0 135.3 jit_solution(13954202657347801159)
XLA Ops:
  0.6 3.1 %edges.1 = bf16[128,4,768]{2,1,0:T(4,128)(2,1)} custom-call(bf16[36,36,128]{2,1,0:T(8,128)(2,1)} %pair_hbm.3, bf16[128,640]{1,0:T(8,128)(2,1)} %w_hbm.3, f32[1,128]{1,0:T(1,128)} %bitcast.14, f32[1,128]{1,0:T(1,128)} %bitcast.16), custom_call_target="tpu_custom_call" | custom-call | flops 200000000 | bytes 1200000 | tf_op jit(solution)/shard_map/edges/pallas_call | solution.py:204
  3.8 16.4 %all-to-all-start = ((bf16[128,4,768]{2,1,0:T(4,128)(2,1)}), bf16[128,4,768]{2,1,0:T(4,128)(2,1)S(1)}, u32[]{:S(2)}, u32[]{:S(2)}) async-start(bf16[128,4,768]{2,1,0:T(4,128)(2,1)} %edges.1), calls=%async_computation | async-start | bytes 1572864 | tf_op jit(solution)/shard_map/all_to_all | solution.py:568
  20.1 4.4 %side.1 = (f32[12,128,128]{2,1,0:T(8,128)S(1)}, f32[12,128,128]{2,1,0:T(8,128)S(1)}, f32[12,128,128]{2,1,0:T(8,128)S(1)}, bf16[12,512,128]{2,1,0:T(8,128)(2,1)S(...) custom-call(bf16[36,36,128]{2,1,0:T(8,128)(2,1)} %pair_hbm.3, ...), custom_call_target="tpu_custom_call" | custom-call | flops 300000000 | bytes 6000000 | tf_op jit(solution)/shard_map/side/pallas_call | solution.py:272
  24.5 1.2 copy-done
  25.7 0.9 copy-done.2
  26.6 0.9 copy-done.4
  27.5 0.9 copy-done.6
  28.4 0.7 copy-done.8
  29.0 14.7 %all-to-all-done = bf16[128,4,768]{2,1,0:T(4,128)(2,1)S(1)} async-done(((bf16[128,4,768]{2,1,0:T(4,128)(2,1)}), bf16[128,4,768]{2,1,0:T(4,128)(2,1)S(1)}, u32[]{:S(2)}, u32[]{:S(2)}) %all-to-all-start) | async-done | bytes 786464 | tf_op jit(solution)/shard_map/all_to_all | solution.py:568
  43.7 0.6 assemble_right.1.right_ref.own_ref
  44.3 3.6 %collective-permute-start = (bf16[384,768]{1,0:T(8,128)(2,1)S(1)}, bf16[384,768]{1,0:T(8,128)(2,1)S(1)}, u32[]{:S(2)}, u32[]{:S(2)}) collective-permute-start(bf16[384,768]{1,0:T(8,128)(2,1)S(1)} %assemble_right.1.right_ref.own_ref), channel_id=1, source_target_pairs={{0,16},{16,0},{1,17},{17,1},{2,18},{18,2},{3,19},{19,3},{4,20},{20... | collective-permute-start | bytes 1769480 | tf_op jit(solution)/shard_map/ppermute | solution.py:572
  47.9 0.5 assemble_left.1.left_ref.left_own_ref
  48.5 0.7 products_own.1.own_ref
  49.2 0.4 collective-permute-done.right_ref.other_ref
  49.5 0.7 products.1
  50.6 22.1 %all_to_all.20.prod_ref = bf16[128,4,384]{2,1,0:T(4,128)(2,1)S(1)} all-to-all(bf16[128,4,384]{2,1,0:T(4,128)(2,1)S(1)} %bitcast.12), channel_id=1, replica_groups=mesh['zh'=2,'x'=4,'core'=2,'y'=4,'zl'=4] {'zh','zl','x','y'}, dimensions={0} | all-to-all | bytes 786432 | tf_op jit(solution)/shard_map/all_to_all | solution.py:568
  72.7 1.2 middle.1
  74.0 21.3 %all_to_all.21 = bf16[128,4,384]{2,1,0:T(4,128)(2,1)S(1)} all-to-all(bf16[128,4,384]{2,1,0:T(4,128)(2,1)S(1)} %get-tuple-element.49), channel_id=1, replica_groups=mesh['zh'=2,'x'=4,'core'=2,'y'=4,'zl'=4] {'zh','zl','x','y'}, dimensions={0} | all-to-all | bytes 786432 | tf_op jit(solution)/shard_map/all_to_all | solution.py:568
  95.2 0.5 regroup.1
  95.8 3.9 %collective-permute-start.2 = (bf16[384,384]{1,0:T(8,128)(2,1)S(1)}, bf16[384,384]{1,0:T(8,128)(2,1)S(1)}, u32[]{:S(2)}, u32[]{:S(2)}) collective-permute-start(bf16[384,384]{1,0:T(8,128)(2,1)S(1)} %get-tuple-element.51.send_ref), channel_id=1, source_target_pairs={{0,16},{16,0},{1,17},{17,1},{2,18},{18,2},{3,19},{19,3},{4,20},{20... | collective-permute-start | bytes 884744 | tf_op jit(solution)/shard_map/ppermute | solution.py:572
  99.6 2.3 %left_grad.1 = (bf16[2,4,4,4,4,384]{5,4,3,2,1,0:T(4,128)(2,1)S(1)}, bf16[384,768]{1,0:T(8,128)(2,1)S(1)}, f32[384,768]{1,0:T(8,128)S(1)}) custom-call(bf16[384,384]{1,0:T(8,128)(2,1)S(1)} %get-tuple-element.50.keep_ref, bf16[384,384]{1,0:T(8,128)(2,1)S(1)} %get-tuple-element.51.send_ref, bf16[384,768]{1,0:T(8,128)(2,1)S(1)} %assemble_right.1.right_ref.own_ref, ...), custom_call_target="tpu_custom_call" | custom-call | flops 450000000 | bytes 2200000 | tf_op jit(solution)/shard_map/left_grad/pallas_call | solution.py:478
  101.9 0.9 right_grad.1
  102.8 30.2 %all_to_all.22.d_ref = bf16[128,4,768]{2,1,0:T(4,128)(2,1)S(1)} all-to-all(bf16[128,4,768]{2,1,0:T(4,128)(2,1)S(1)} %bitcast.13), channel_id=1, replica_groups=mesh['zh'=2,'x'=4,'core'=2,'y'=4,'zl'=4] {'zh','zl','x','y'}, dimensions={0} | all-to-all | bytes 1572864 | tf_op jit(solution)/shard_map/all_to_all | solution.py:568
  133.0 2.1 %finish.1 = bf16[36,36,128]{2,1,0:T(8,128)(2,1)} custom-call(bf16[128,4,768]{2,1,0:T(4,128)(2,1)S(1)} %all_to_all.22.d_ref, bf16[12,512,128]{2,1,0:T(8,128)(2,1)S(1)} %copy-done.1, bf16[12,128,128]{2,1,0:T(8,128)(2,1)S(1)} %get-tuple-element.60.dgate_ref, f32[12,128,128]{2,1,0:T(8,128)S(1)} %copy-done.7, f32[16,128]{1,0:T(8,128)S(1)} %get-tuple-element.62.scale_ref, ...), custom_call_target="tpu_custom_call" | custom-call | flops 250000000 | bytes 4000000 | tf_op jit(solution)/shard_map/finish/pallas_call | solution.py:551
  (18 shorter events, 0.5 us)
Async XLA Ops:
  3.8 39.9 %all-to-all-start = ((bf16[128,4,768]{2,1,0:T(4,128)(2,1)}), bf16[128,4,768]{2,1,0:T(4,128)(2,1)S(1)}, u32[]{:S(2)}, u32[]{:S(2)}) async-start(bf16[128,4,768]{2,1,0:T(4,128)(2,1)} %edges.1), calls=%async_computation | async-start | bytes 1572864 | tf_op jit(solution)/shard_map/all_to_all | solution.py:568
  24.5 1.2 copy-start
  25.7 0.9 copy-start.2
  26.6 0.9 copy-start.4
  27.5 0.9 copy-start.6
  28.4 0.7 copy-start.8
  44.3 5.2 %collective-permute-start = (bf16[384,768]{1,0:T(8,128)(2,1)S(1)}, bf16[384,768]{1,0:T(8,128)(2,1)S(1)}, u32[]{:S(2)}, u32[]{:S(2)}) collective-permute-start(bf16[384,768]{1,0:T(8,128)(2,1)S(1)} %assemble_right.1.right_ref.own_ref), channel_id=1, source_target_pairs={{0,16},{16,0},{1,17},{17,1},{2,18},{18,2},{3,19},{19,3},{4,20},{20... | collective-permute-start | bytes 1769480 | tf_op jit(solution)/shard_map/ppermute | solution.py:572
  48.4 2.2 %collective-permute-start.1 = (bf16[384,768]{1,0:T(8,128)(2,1)S(1)}, bf16[384,768]{1,0:T(8,128)(2,1)}, u32[]{:S(2)}, u32[]{:S(2)}) collective-permute-start(bf16[384,768]{1,0:T(8,128)(2,1)S(1)} %assemble_left.1.left_ref.left_own_ref), channel_id=1, source_target_pairs={{0,16},{16,0},{1,17},{17,1},{2,18},{18,2},{3,19},{19,3},{4,20},{20... | collective-permute-start | bytes 1769480 | tf_op jit(solution)/shard_map/ppermute | solution.py:572
  49.1 23.6 %copy-start.3 = (f32[12,128,128]{2,1,0:T(8,128)S(1)}, f32[12,128,128]{2,1,0:T(8,128)}, u32[]{:S(2)}) copy-start(f32[12,128,128]{2,1,0:T(8,128)} %copy-done.2) | copy-start | bytes 2359300
  49.1 23.6 %copy-start.5 = (f32[12,128,128]{2,1,0:T(8,128)S(1)}, f32[12,128,128]{2,1,0:T(8,128)}, u32[]{:S(2)}) copy-start(f32[12,128,128]{2,1,0:T(8,128)} %copy-done.4) | copy-start | bytes 2359300
  95.8 6.1 %collective-permute-start.2 = (bf16[384,384]{1,0:T(8,128)(2,1)S(1)}, bf16[384,384]{1,0:T(8,128)(2,1)S(1)}, u32[]{:S(2)}, u32[]{:S(2)}) collective-permute-start(bf16[384,384]{1,0:T(8,128)(2,1)S(1)} %get-tuple-element.51.send_ref), channel_id=1, source_target_pairs={{0,16},{16,0},{1,17},{17,1},{2,18},{18,2},{3,19},{19,3},{4,20},{20... | collective-permute-start | bytes 884744 | tf_op jit(solution)/shard_map/ppermute | solution.py:572
  101.9 31.1 %copy-start.1 = (bf16[12,512,128]{2,1,0:T(8,128)(2,1)S(1)}, bf16[12,512,128]{2,1,0:T(8,128)(2,1)}, u32[]{:S(2)}) copy-start(bf16[12,512,128]{2,1,0:T(8,128)(2,1)} %copy-done) | copy-start | bytes 4718596
  101.9 31.1 %copy-start.7 = (f32[12,128,128]{2,1,0:T(8,128)S(1)}, f32[12,128,128]{2,1,0:T(8,128)}, u32[]{:S(2)}) copy-start(f32[12,128,128]{2,1,0:T(8,128)} %copy-done.6) | copy-start | bytes 2359300
  101.9 31.1 %copy-start.9 = (bf16[128,640]{1,0:T(8,128)(2,1)S(1)}, bf16[128,640]{1,0:T(8,128)(2,1)}, u32[]{:S(2)}) copy-start(bf16[128,640]{1,0:T(8,128)(2,1)} %copy-done.8) | copy-start | bytes 491524

commit v3 on v1

--- a/solution.py
+++ b/solution.py
@@ -178,12 +178,13 @@
     wt_scr[...] = w_ref[:, : 4 * CH].astype(F32).T.astype(BF)
     copies[2].wait()
     copies[3].wait()
+    gain, bias = column(gain_ref[...]), column(bias_ref[...])
     copies[0].wait()
     spread_tile(pair_ref, x_scr)
     for r in range(0, GROUPS, 2):
-        xhat, _ = normalized(x_scr[r : r + 2].reshape(2 * LANES, CH), 1)
-        normed = (xhat * gain_ref[...] + bias_ref[...]).astype(BF)
-        proj = dot(wt_scr[...], normed, 1, 1)
+        xhat, _ = normalized(jnp.concatenate([x_scr[r].T, x_scr[r + 1].T], 1), 0)
+        normed = (xhat * gain + bias).astype(BF)
+        proj = dot(wt_scr[...], normed, 1, 0)
         left = jax.nn.sigmoid(proj[:CH]) * proj[CH : 2 * CH]
         right = jax.nn.sigmoid(proj[2 * CH : 3 * CH]) * proj[3 * CH :]
         for n in (r, r + 1):

time: 136 us -> 136 us (level)
  no operation moved by 1% of the time
where the time goes in v3:
time: 136 us; the launch traced here: 135 us
  blocking collectives  73.6 us (54%)
  starting transfers between devices  23.9 us (18%)
  Pallas kernels  17.1 us (13%)
  waiting for transfers between devices  15.4 us (11%)
  local copies, waits for them, and re-layouts  4.52 us (3%)
    all_to_all x3, blocking collectives, exchange(): return lax.all_to_all(x, WIDE, 0, 0, tiled=True)  73.6 us
    all_to_all x1, starting transfers between devices, exchange(): return lax.all_to_all(x, WIDE, 0, 0, tiled=True)  16.4 us
    all_to_all x1, waiting for transfers between devices, exchange(): return lax.all_to_all(x, WIDE, 0, 0, tiled=True)  14.7 us
    ppermute x3, starting transfers between devices, other_core(): return lax.ppermute(x, 'core', [(0, 1), (1, 0)])  7.52 us
    unnamed x20, local copies, waits for them, and re-layouts  4.52 us
    pallas_call x1, Pallas kernels, side(): pl.pallas_call(side_kernel, out_shape=[square, square, square, jax.ShapeD...  4.39 us
    pallas_call x1, Pallas kernels, edges(): pl.pallas_call(edges_kernel, out_shape=message((CH,), 2), in_specs=in_hbm...  3.22 us
  transfers between devices with their start and end apart: 4, of which 3 were waited for; matrix products, arithmetic and copies ran while one was open for 0% of the time, Pallas kernels for 6%

profile of v3, /device:TPU:1, one launch (start us, length us, event | category | flops | bytes accessed | tf_op | source)
XLA Modules:
  0.0 135.5 jit_solution(419110552065877686)
XLA Ops:
  0.6 3.2 %edges.1 = bf16[128,4,768]{2,1,0:T(4,128)(2,1)} custom-call(bf16[36,36,128]{2,1,0:T(8,128)(2,1)} %pair_hbm.3, bf16[128,640]{1,0:T(8,128)(2,1)} %w_hbm.3, f32[1,128]{1,0:T(1,128)} %bitcast.14, f32[1,128]{1,0:T(1,128)} %bitcast.16), custom_call_target="tpu_custom_call" | custom-call | flops 200000000 | bytes 1200000 | tf_op jit(solution)/shard_map/edges/pallas_call | solution.py:205
  3.9 16.4 %all-to-all-start = ((bf16[128,4,768]{2,1,0:T(4,128)(2,1)}), bf16[128,4,768]{2,1,0:T(4,128)(2,1)S(1)}, u32[]{:S(2)}, u32[]{:S(2)}) async-start(bf16[128,4,768]{2,1,0:T(4,128)(2,1)} %edges.1), calls=%async_computation | async-start | bytes 1572864 | tf_op jit(solution)/shard_map/all_to_all | solution.py:564
  20.2 4.4 %side.1 = (f32[12,128,128]{2,1,0:T(8,128)S(1)}, f32[12,128,128]{2,1,0:T(8,128)S(1)}, f32[12,128,128]{2,1,0:T(8,128)S(1)}, bf16[12,512,128]{2,1,0:T(8,128)(2,1)S(...) custom-call(bf16[36,36,128]{2,1,0:T(8,128)(2,1)} %pair_hbm.3, ...), custom_call_target="tpu_custom_call" | custom-call | flops 300000000 | bytes 6000000 | tf_op jit(solution)/shard_map/side/pallas_call | solution.py:273
  24.6 1.2 copy-done
  25.8 0.9 copy-done.2
  26.7 0.9 copy-done.4
  27.6 0.9 copy-done.6
  28.5 0.7 copy-done.8
  29.1 14.7 %all-to-all-done = bf16[128,4,768]{2,1,0:T(4,128)(2,1)S(1)} async-done(((bf16[128,4,768]{2,1,0:T(4,128)(2,1)}), bf16[128,4,768]{2,1,0:T(4,128)(2,1)S(1)}, u32[]{:S(2)}, u32[]{:S(2)}) %all-to-all-start) | async-done | bytes 786464 | tf_op jit(solution)/shard_map/all_to_all | solution.py:564
  43.8 0.6 assemble_right.1.right_ref.own_ref
  44.4 3.6 %collective-permute-start = (bf16[384,768]{1,0:T(8,128)(2,1)S(1)}, bf16[384,768]{1,0:T(8,128)(2,1)S(1)}, u32[]{:S(2)}, u32[]{:S(2)}) collective-permute-start(bf16[384,768]{1,0:T(8,128)(2,1)S(1)} %assemble_right.1.right_ref.own_ref), channel_id=1, source_target_pairs={{0,16},{16,0},{1,17},{17,1},{2,18},{18,2},{3,19},{19,3},{4,20},{20... | collective-permute-start | bytes 1769480 | tf_op jit(solution)/shard_map/ppermute | solution.py:568
  48.0 0.5 assemble_left.1.left_ref
  48.5 0.7 products_own.1.own_ref
  49.2 0.4 collective-permute-done.right_ref.other_ref
  49.6 0.7 products.1
  50.7 22.1 %all_to_all.20.prod_ref = bf16[128,4,384]{2,1,0:T(4,128)(2,1)S(1)} all-to-all(bf16[128,4,384]{2,1,0:T(4,128)(2,1)S(1)} %bitcast.12), channel_id=1, replica_groups=mesh['zh'=2,'x'=4,'core'=2,'y'=4,'zl'=4] {'zh','zl','x','y'}, dimensions={0} | all-to-all | bytes 786432 | tf_op jit(solution)/shard_map/all_to_all | solution.py:564
  72.8 1.2 middle.1
  74.0 21.3 %all_to_all.21 = bf16[128,4,384]{2,1,0:T(4,128)(2,1)S(1)} all-to-all(bf16[128,4,384]{2,1,0:T(4,128)(2,1)S(1)} %get-tuple-element.48), channel_id=1, replica_groups=mesh['zh'=2,'x'=4,'core'=2,'y'=4,'zl'=4] {'zh','zl','x','y'}, dimensions={0} | all-to-all | bytes 786432 | tf_op jit(solution)/shard_map/all_to_all | solution.py:564
  95.3 0.5 regroup.1
  95.8 3.8 %collective-permute-start.2 = (bf16[384,384]{1,0:T(8,128)(2,1)S(1)}, bf16[384,384]{1,0:T(8,128)(2,1)S(1)}, u32[]{:S(2)}, u32[]{:S(2)}) collective-permute-start(bf16[384,384]{1,0:T(8,128)(2,1)S(1)} %get-tuple-element.50.send_ref), channel_id=1, source_target_pairs={{0,16},{16,0},{1,17},{17,1},{2,18},{18,2},{3,19},{19,3},{4,20},{20... | collective-permute-start | bytes 884744 | tf_op jit(solution)/shard_map/ppermute | solution.py:568
  99.7 2.1 %left_grad.1 = (bf16[2,4,4,4,4,384]{5,4,3,2,1,0:T(4,128)(2,1)S(1)}, bf16[384,768]{1,0:T(8,128)(2,1)S(1)}) custom-call(bf16[384,384]{1,0:T(8,128)(2,1)S(1)} %get-tuple-element.49.keep_ref, bf16[384,384]{1,0:T(8,128)(2,1)S(1)} %get-tuple-element.50.send_ref, bf16[384,768]{1,0:T(8,128)(2,1)S(1)} %assemble_right.1.right_ref.own_ref, ...), custom_call_target="tpu_custom_call" | custom-call | flops 450000000 | bytes 2200000 | tf_op jit(solution)/shard_map/left_grad/pallas_call | solution.py:476
  101.8 1.2 right_grad.1
  103.0 30.2 %all_to_all.22.d_ref = bf16[128,4,768]{2,1,0:T(4,128)(2,1)S(1)} all-to-all(bf16[128,4,768]{2,1,0:T(4,128)(2,1)S(1)} %bitcast.13), channel_id=1, replica_groups=mesh['zh'=2,'x'=4,'core'=2,'y'=4,'zl'=4] {'zh','zl','x','y'}, dimensions={0} | all-to-all | bytes 1572864 | tf_op jit(solution)/shard_map/all_to_all | solution.py:564
  133.2 2.1 %finish.1 = bf16[36,36,128]{2,1,0:T(8,128)(2,1)} custom-call(bf16[128,4,768]{2,1,0:T(4,128)(2,1)S(1)} %all_to_all.22.d_ref, bf16[12,512,128]{2,1,0:T(8,128)(2,1)S(1)} %copy-done.1, bf16[12,128,128]{2,1,0:T(8,128)(2,1)S(1)} %get-tuple-element.58.dgate_ref, f32[12,128,128]{2,1,0:T(8,128)S(1)} %copy-done.7, f32[16,128]{1,0:T(8,128)S(1)} %get-tuple-element.60.scale_ref, ...), custom_call_target="tpu_custom_call" | custom-call | flops 250000000 | bytes 4000000 | tf_op jit(solution)/shard_map/finish/pallas_call | solution.py:547
  (18 shorter events, 0.5 us)
Async XLA Ops:
  3.9 39.9 %all-to-all-start = ((bf16[128,4,768]{2,1,0:T(4,128)(2,1)}), bf16[128,4,768]{2,1,0:T(4,128)(2,1)S(1)}, u32[]{:S(2)}, u32[]{:S(2)}) async-start(bf16[128,4,768]{2,1,0:T(4,128)(2,1)} %edges.1), calls=%async_computation | async-start | bytes 1572864 | tf_op jit(solution)/shard_map/all_to_all | solution.py:564
  24.6 1.2 copy-start
  25.8 0.9 copy-start.2
  26.7 0.9 copy-start.4
  27.6 0.9 copy-start.6
  28.5 0.7 copy-start.8
  44.4 5.2 %collective-permute-start = (bf16[384,768]{1,0:T(8,128)(2,1)S(1)}, bf16[384,768]{1,0:T(8,128)(2,1)S(1)}, u32[]{:S(2)}, u32[]{:S(2)}) collective-permute-start(bf16[384,768]{1,0:T(8,128)(2,1)S(1)} %assemble_right.1.right_ref.own_ref), channel_id=1, source_target_pairs={{0,16},{16,0},{1,17},{17,1},{2,18},{18,2},{3,19},{19,3},{4,20},{20... | collective-permute-start | bytes 1769480 | tf_op jit(solution)/shard_map/ppermute | solution.py:568
  48.4 2.2 %collective-permute-start.1 = (bf16[384,768]{1,0:T(8,128)(2,1)S(1)}, bf16[384,768]{1,0:T(8,128)(2,1)}, u32[]{:S(2)}, u32[]{:S(2)}) collective-permute-start(bf16[384,768]{1,0:T(8,128)(2,1)S(1)} %assemble_left.1.left_ref), channel_id=1, source_target_pairs={{0,16},{16,0},{1,17},{17,1},{2,18},{18,2},{3,19},{19,3},{4,20},{20... | collective-permute-start | bytes 1769480 | tf_op jit(solution)/shard_map/ppermute | solution.py:568
  49.2 23.6 %copy-start.3 = (f32[12,128,128]{2,1,0:T(8,128)S(1)}, f32[12,128,128]{2,1,0:T(8,128)}, u32[]{:S(2)}) copy-start(f32[12,128,128]{2,1,0:T(8,128)} %copy-done.2) | copy-start | bytes 2359300
  49.2 23.6 %copy-start.5 = (f32[12,128,128]{2,1,0:T(8,128)S(1)}, f32[12,128,128]{2,1,0:T(8,128)}, u32[]{:S(2)}) copy-start(f32[12,128,128]{2,1,0:T(8,128)} %copy-done.4) | copy-start | bytes 2359300
  95.8 5.9 %collective-permute-start.2 = (bf16[384,384]{1,0:T(8,128)(2,1)S(1)}, bf16[384,384]{1,0:T(8,128)(2,1)S(1)}, u32[]{:S(2)}, u32[]{:S(2)}) collective-permute-start(bf16[384,384]{1,0:T(8,128)(2,1)S(1)} %get-tuple-element.50.send_ref), channel_id=1, source_target_pairs={{0,16},{16,0},{1,17},{17,1},{2,18},{18,2},{3,19},{19,3},{4,20},{20... | collective-permute-start | bytes 884744 | tf_op jit(solution)/shard_map/ppermute | solution.py:568
  101.8 31.4 %copy-start.1 = (bf16[12,512,128]{2,1,0:T(8,128)(2,1)S(1)}, bf16[12,512,128]{2,1,0:T(8,128)(2,1)}, u32[]{:S(2)}) copy-start(bf16[12,512,128]{2,1,0:T(8,128)(2,1)} %copy-done) | copy-start | bytes 4718596
  101.8 31.4 %copy-start.7 = (f32[12,128,128]{2,1,0:T(8,128)S(1)}, f32[12,128,128]{2,1,0:T(8,128)}, u32[]{:S(2)}) copy-start(f32[12,128,128]{2,1,0:T(8,128)} %copy-done.6) | copy-start | bytes 2359300
  101.8 31.4 %copy-start.9 = (bf16[128,640]{1,0:T(8,128)(2,1)S(1)}, bf16[128,640]{1,0:T(8,128)(2,1)}, u32[]{:S(2)}) copy-start(bf16[128,640]{1,0:T(8,128)(2,1)} %copy-done.8) | copy-start | bytes 491524
